TPU v7x, 256 devices: a whole 4x4x8 slice. The times are simulated.
256 devices in a mesh: dp: 16 (over y, x), ctx: 16 (over z, core).
Axes of the slice: x: 4, y: 4, z: 8, core: 2. Of those that a mesh axis runs over, the one named last changes fastest.
Arguments:
- frames: bfloat16 [8192, 6144], P('ctx'), may hold values from -6 to 6
- proj_weight: bfloat16 [3, 6144, 4096], P(None, 'ctx', 'dp'), may hold values from -0.078125 to 0.078125
- out_weight: bfloat16 [6144, 4096], P('dp', 'ctx'), may hold values from -0.09375 to 0.09375
- query_gain: float32 [4096], P('dp'), may hold values from 0.5 to 2
- key_gain: float32 [4096], P('dp'), may hold values from 0.5 to 2
- key_tiles: int32 [32, 128, 18], P('dp', 'ctx'), may hold values from 0 to 127, as said below
- key_counts: int32 [32, 128], P('dp', 'ctx'), may hold values from 1 to 18
Outputs:
- mixed: bfloat16 [8192, 6144], P('ctx', 'dp')
Inputs may be any that keep to these rules, and one draw needn't show every extreme that they name: `key_tiles`: tiles have coordinates (frame layer, height, width) on a grid of 16 x 2 x 4, tile number (layer * 2 + height) * 4 + width. For each head and query tile, the first key_counts entries are distinct tiles that differ from the query tile by at most one in each coordinate, the query tile itself among them; the other entries repeat the query tile. In every head some tile lists its whole window.
All inputs are finite; a program needn't handle non-finite values.
Results may differ from a plain program's by a relative error of at most 0.0088.
Values may be sent and summed in bfloat16 or wider, within the bound.
A program may use at most 64 MiB of HBM per device.

v0:
```python
import jax
import jax.numpy as jnp
from jax import lax
from jax.sharding import PartitionSpec as P

TILE = 64
eps = 1e-06


def padded(block, sides, width):
    for axis, dim in sides:
        count = lax.axis_size(axis)
        forward = [(i, i + 1) for i in range(count - 1)]
        backward = [(target, source) for source, target in forward]
        low = lax.ppermute(
            lax.slice_in_dim(block, block.shape[dim] - width, None, axis=dim), axis, forward
        )
        high = lax.ppermute(lax.slice_in_dim(block, 0, width, axis=dim), axis, backward)
        block = jnp.concatenate([low, block, high], axis=dim)
    return block


def normed(rows, gain):
    stat = jnp.mean(rows * rows, axis=-1, keepdims=True)
    return rows * lax.rsqrt(stat + eps) * gain


def attend(query_rows, key_rows, value_rows, tile_ids, tile_counts, first_tile):
    heads = tile_ids.shape[0]
    slots = tile_ids.shape[2]
    head_dim = query_rows.shape[1] // heads
    query_tiles = query_rows.reshape(-1, TILE, heads, head_dim).transpose(2, 0, 1, 3)
    key_tiles = key_rows.reshape(-1, TILE, heads, head_dim).transpose(2, 0, 1, 3)
    value_tiles = value_rows.reshape(-1, TILE, heads, head_dim).transpose(2, 0, 1, 3)
    local_ids = tile_ids - first_tile
    picked_keys = jax.vmap(lambda lookup, indices: lookup[indices])(key_tiles, local_ids)
    picked_values = jax.vmap(lambda lookup, indices: lookup[indices])(value_tiles, local_ids)
    count_q = query_tiles.shape[1]
    picked_keys = picked_keys.reshape(heads, count_q, slots * TILE, head_dim)
    picked_values = picked_values.reshape(heads, count_q, slots * TILE, head_dim)
    scores = jnp.einsum(
        "hqtd,hqsd->hqts", query_tiles, picked_keys, preferred_element_type=jnp.float32
    ) * head_dim ** (-0.5)
    live = (jnp.arange(slots, dtype=jnp.int32)[None, None, :] < tile_counts[:, :, None]).astype(
        jnp.float32
    )
    live = jnp.repeat(live, TILE, axis=2)[:, :, None, :]
    weights = jnp.exp(scores) * live
    totals = jnp.sum(weights, axis=-1, keepdims=True)
    summed = (
        jnp.einsum(
            "hqts,hqsd->hqtd",
            weights.astype(jnp.bfloat16),
            picked_values,
            preferred_element_type=jnp.float32,
        )
        / totals
    )
    return summed.astype(jnp.bfloat16).transpose(1, 2, 0, 3).reshape(-1, heads * head_dim)


def body(frames, proj_weight, out_weight, query_gain, key_gain, key_tiles, key_counts):
    heads = key_tiles.shape[0]
    width = proj_weight.shape[2]
    head_dim = width // heads
    layer_tiles = key_tiles.shape[1]
    tok_count = frames.shape[0]
    columns = frames
    proj = jnp.einsum(
        "tn,cnw->ctw",
        columns,
        lax.all_gather(proj_weight, "ctx", axis=1, tiled=True),
        preferred_element_type=jnp.float32,
    )
    query_rows = normed(proj[0].reshape(-1, heads, head_dim), query_gain.reshape(heads, head_dim))
    key_rows = normed(proj[1].reshape(-1, heads, head_dim), key_gain.reshape(heads, head_dim))
    query_rows = query_rows.reshape(-1, width).astype(jnp.bfloat16)
    key_rows = key_rows.reshape(-1, width).astype(jnp.bfloat16)
    value_rows = proj[2].astype(jnp.bfloat16)
    paired = jnp.stack([key_rows, value_rows], axis=0)
    widened = padded(paired, (("ctx", 1),), tok_count)
    first_tile = (lax.axis_index("ctx") - 1) * layer_tiles
    attended = attend(query_rows, widened[0], widened[1], key_tiles, key_counts, first_tile)
    out_columns = lax.all_gather(out_weight, "ctx", axis=1, tiled=True)
    columns = out_columns
    mixed = lax.dot_general(
        lax.all_gather(attended, "dp", axis=1, tiled=True),
        columns,
        (((1,), (1,)), ((), ())),
        preferred_element_type=jnp.float32,
    )
    return mixed.astype(jnp.bfloat16)


def solution(mesh):
    placed = (
        P("ctx", None),
        P(None, "ctx", "dp"),
        P("dp", "ctx"),
        P("dp"),
        P("dp"),
        P("dp", "ctx", None),
        P("dp", "ctx"),
    )
    return jax.shard_map(
        body, mesh=mesh, in_specs=placed, out_specs=P("ctx", "dp"), check_vma=False
    )
```

profile of v0, /device:TPU:1, one launch (start us, length us, event | category | flops | bytes accessed | tf_op | source)
XLA Modules:
  0.0 201.2 jit_solution(7556137137856312792)
XLA Ops:
  6.5 0.0 all-gather.4.cloned.1.call-start
  6.5 2.1 %copy.12 = bf16[3,384,256]{1,2,0:T(8,128)(2,1)} copy(bf16[3,384,256]{2,1,0:T(8,128)(2,1)} %param.8) | data formatting | bytes 1179648 | tf_op args[1]
  8.7 0.0 all-gather.4.cloned.1.call-update
  8.7 0.0 all-gather.8.cloned.1.call-start
  8.8 0.7 all-gather.8.cloned.1.call-update
  9.5 0.0 all-gather.6.cloned.1.call-start
  9.5 0.7 fusion.23
  10.2 0.0 copy-start.1
  10.2 64.0 %all-gather.4.cloned.1.call-done = bf16[3,6144,256]{1,2,0:T(8,128)(2,1)} async-done(((bf16[3,384,256]{1,2,0:T(8,128)(2,1)}), bf16[3,6144,256]{1,2,0:T(8,128)(2,1)}) %all-gather.4.cloned.1.call-update) | async-done | bytes 9437200 | tf_op jit(solution)/shard_map/all_gather | solution.py:72
  74.2 9.5 %fusion.4 = f32[3,512,256]{1,2,0:T(8,128)S(1)} fusion(bf16[3,6144,256]{1,2,0:T(8,128)(2,1)} %all-gather.4.cloned.1.call-done, bf16[512,6144]{1,0:T(8,128)(2,1)} %param.7), kind=kOutput, calls=%fused_computation.9 | convolution fusion | flops 4831838208 | bytes 17301504 | tf_op jit(solution)/shard_map/tn,cnw->ctw/dot_general | solution.py:69
  83.7 0.0 copy-start.3
  83.8 0.0 copy-start.2
  83.8 0.1 reduce_sum.28
  83.9 0.0 copy-done.1
  83.9 0.2 slice_multiply_fusion.1
  84.1 0.1 pad_maximum_fusion.1
  84.2 1.9 collective-permute-start
  86.1 3.4 %collective-permute-start.1 = (bf16[2,512,256]{1,2,0:T(8,128)(2,1)S(1)}, bf16[2,512,256]{1,2,0:T(8,128)(2,1)}, u32[]{:S(2)}, u32[]{:S(2)}) collective-permute-start(bf16[2,512,256]{1,2,0:T(8,128)(2,1)S(1)} %pad_maximum_fusion.1), channel_id=1, source_target_pairs={{1,0},{2,1},{3,2},{4,3},{5,4},{6,5},{7,6},{8,7},{9,8},{10,9},{11,1... | collective-permute-start | bytes 1572872 | tf_op jit(solution)/shard_map/ppermute | solution.py:18
  89.5 0.0 copy-done.3
  89.5 0.1 fusion.24
  89.5 0.1 reshape.68
  89.6 0.1 broadcast_in_dim.5
  89.7 0.1 mul.100
  89.8 0.2 copy.13
  90.0 0.3 reshape_squeeze.10
  90.3 0.1 reduce_sum.27
  90.4 0.1 copy.14
  90.6 0.0 copy-done.2
  90.6 0.7 fusion.18
  91.3 3.3 %collective-permute-done = bf16[2,512,256]{1,2,0:T(8,128)(2,1)} collective-permute-done((bf16[2,512,256]{1,2,0:T(8,128)(2,1)S(1)}, bf16[2,512,256]{1,2,0:T(8,128)(2,1)}, u32[]{:S(2)}, u32[]{:S(2)}) %collective-permute-start) | collective-permute-done | bytes 524320 | tf_op jit(solution)/shard_map/ppermute | solution.py:15
  94.6 4.4 %collective-permute-done.1 = bf16[2,512,256]{1,2,0:T(8,128)(2,1)} collective-permute-done((bf16[2,512,256]{1,2,0:T(8,128)(2,1)S(1)}, bf16[2,512,256]{1,2,0:T(8,128)(2,1)}, u32[]{:S(2)}, u32[]{:S(2)}) %collective-permute-start.1) | collective-permute-done | bytes 524320 | tf_op jit(solution)/shard_map/ppermute | solution.py:18
  99.0 1.3 pad_maximum_fusion
  100.3 1.0 fusion.25
  101.3 0.9 reshape.88
  102.2 1.0 copy.16
  103.2 2.4 %reshape.89 = bf16[24,64,2,128]{1,0,3,2:T(8,128)(2,1)S(1)} reshape(bf16[1,1536,256]{1,2,0:T(8,128)(2,1)} %get-tuple-element.9) | data formatting | bytes 1572864 | tf_op jit(solution)/shard_map/reshape;squeeze | solution.py:34
  105.6 1.0 copy.19
  106.6 6.4 %gather_fusion = bf16[288,64,128]{2,1,0:T(8,128)(2,1)} fusion(bf16[2,24,64,128]{3,2,1,0:T(8,128)(2,1)S(1)} %bitcast.53, s32[288]{0:T(512)S(1)} %reshape.68), kind=kCustom, calls=%fused_computation | custom fusion | bytes 9439488 | tf_op jit(solution)/shard_map/vmap()/gather | solution.py:36
  113.0 6.3 %gather_fusion.1 = bf16[288,64,128]{2,1,0:T(8,128)(2,1)} fusion(bf16[2,24,64,128]{3,2,1,0:T(8,128)(2,1)S(1)} %bitcast.54, s32[288]{0:T(512)S(1)} %reshape.68), kind=kCustom, calls=%fused_computation.1 | custom fusion | bytes 9439488 | tf_op jit(solution)/shard_map/vmap()/gather | solution.py:37
  119.3 4.5 %fusion.26 = (f32[2,8,64]{2,1,0:T(8,128)S(1)}, bf16[2,8,64,1152]{3,2,1,0:T(8,128)(2,1)S(1)}) fusion(f32[2,8,1152]{2,1,0:T(8,128)S(1)} %mul.100, bf16[2,8,1152,128]{3,2,1,0:T(8,128)(2,1)} %bitcast.56, bf16[2,8,64,128]{3,0,2,1:T(2,128)(2,1)S(1)} %fusion.18), kind=kOutput, calls=%fused_computation.35 | convolution fusion | flops 306707456 | bytes 7417856 | tf_op jit(solution)/shard_map/hqtd,hqsd->hqts/dot_general | solution.py:41
  123.8 0.0 copy-done
  123.8 1.1 fusion.13
  124.9 0.3 copy.20
  125.2 0.7 copy.31
  125.9 0.0 all-gather.6.cloned.1.call-update
  126.0 0.0 all-gather.8.cloned.1.call-done
  126.0 62.4 %all-gather.6.cloned.1.call-done = bf16[512,4096]{1,0:T(8,128)(2,1)} async-done(((bf16[512,256]{1,0:T(8,128)(2,1)}), bf16[512,4096]{1,0:T(8,128)(2,1)}) %all-gather.6.cloned.1.call-update) | async-done | bytes 4194320 | tf_op jit(solution)/shard_map/all_gather | solution.py:87
  188.4 6.3 %convolution_convert_fusion = bf16[512,384]{1,0:T(8,128)(2,1)} fusion(bf16[512,4096]{1,0:T(8,128)(2,1)} %all-gather.6.cloned.1.call-done, bf16[384,4096]{1,0:T(8,128)(2,1)} %all-gather.8.cloned.1.call-done), kind=kOutput, calls=%fused_computation.10 | convolution fusion | flops 1610809344 | bytes 7733248 | tf_op jit(solution)/shard_map/dot_general | solution.py:86
  (5 shorter events, 0.1 us)
Async XLA Ops:
  6.5 67.6 %all-gather.4.cloned.1.call-start = ((), (), s32[]{:S(2)}) async-start(), calls=%async_computation | async-start | bytes 10027008 | tf_op jit(solution)/shard_map/all_gather | solution.py:72
  8.7 117.3 %all-gather.8.cloned.1.call-start = ((), (), s32[]{:S(2)}) async-start(), calls=%async_computation.2 | async-start | bytes 3342336 | tf_op jit(solution)/shard_map/all_gather | solution.py:84
  9.5 178.9 %all-gather.6.cloned.1.call-start = ((), (), s32[]{:S(2)}) async-start(), calls=%async_computation.1 | async-start | bytes 4456448 | tf_op jit(solution)/shard_map/all_gather | solution.py:87
  10.2 73.7 %copy-start.1 = (f32[256]{0:T(256)S(1)}, f32[256]{0:T(256)}, u32[]{:S(2)}) copy-start(f32[256]{0:T(256)} %param.11) | copy-start | bytes 3076
  83.7 5.8 %copy-start.3 = (s32[2,8]{1,0:T(2,128)S(1)}, s32[2,8]{1,0:T(2,128)}, u32[]{:S(2)}) copy-start(s32[2,8]{1,0:T(2,128)} %param.13) | copy-start | bytes 196
  83.8 6.8 %copy-start.2 = (f32[256]{0:T(256)S(1)}, f32[256]{0:T(256)}, u32[]{:S(2)}) copy-start(f32[256]{0:T(256)} %param.10) | copy-start | bytes 3076
  84.2 10.4 %collective-permute-start = (bf16[2,512,256]{1,2,0:T(8,128)(2,1)S(1)}, bf16[2,512,256]{1,2,0:T(8,128)(2,1)}, u32[]{:S(2)}, u32[]{:S(2)}) collective-permute-start(bf16[2,512,256]{1,2,0:T(8,128)(2,1)S(1)} %pad_maximum_fusion.1), channel_id=1, source_target_pairs={{0,1},{1,2},{2,3},{3,4},{4,5},{5,6},{6,7},{7,8},{8,9},{9,10},{10,1... | collective-permute-start | bytes 1572872 | tf_op jit(solution)/shard_map/ppermute | solution.py:15
  86.1 12.9 %collective-permute-start.1 = (bf16[2,512,256]{1,2,0:T(8,128)(2,1)S(1)}, bf16[2,512,256]{1,2,0:T(8,128)(2,1)}, u32[]{:S(2)}, u32[]{:S(2)}) collective-permute-start(bf16[2,512,256]{1,2,0:T(8,128)(2,1)S(1)} %pad_maximum_fusion.1), channel_id=1, source_target_pairs={{1,0},{2,1},{3,2},{4,3},{5,4},{6,5},{7,6},{8,7},{9,8},{10,9},{11,1... | collective-permute-start | bytes 1572872 | tf_op jit(solution)/shard_map/ppermute | solution.py:18
  119.3 4.5 %copy-start = (bf16[288,64,128]{2,1,0:T(8,128)(2,1)S(1)}, bf16[288,64,128]{2,1,0:T(8,128)(2,1)}, u32[]{:S(2)}) copy-start(bf16[288,64,128]{2,1,0:T(8,128)(2,1)} %gather_fusion.1) | copy-start | bytes 14155780
Sparse Core Ops, SparseCore 0:
  9.1 64.9 all-gather.3
  75.9 45.6 all-gather.7
  126.1 62.2 all-gather.5
where the time goes:
time: 202 us; the launch traced here: 201 us
  waiting for transfers between devices  135 us (67%)
  local copies, waits for them, and re-layouts  23 us (11%)
  matrix products  21.4 us (11%)
  between operations  13.3 us (7%)
  starting transfers between devices  5.36 us (3%)
  other arithmetic  3.22 us (2%)
    all_gather x1, waiting for transfers between devices, body(): lax.all_gather(proj_weight, 'ctx', axis=1, tiled=True)  64 us
    all_gather x1, waiting for transfers between devices, body(): lax.all_gather(attended, 'dp', axis=1, tiled=True)  62.4 us
    gather x3, local copies, waits for them, and re-layouts, attend(): lookup[indices]  12.7 us
    dot_general x1, matrix products, body(): jnp.einsum('tn,cnw->ctw', columns, lax.all_gather(proj_weight, 'ctx', axi...  9.52 us
    dot_general x1, matrix products, body(): lax.dot_general(lax.all_gather(attended, 'dp', axis=1, tiled=True), colum...  6.26 us
    dot_general x1, matrix products, attend(): jnp.einsum('hqtd,hqsd->hqts', query_tiles, picked_keys, preferred_element...  4.49 us
    ppermute x1, waiting for transfers between devices, padded(): lax.ppermute(lax.slice_in_dim(block, 0, width, axis=dim), axis, backward)  4.43 us
  transfers between devices with their start and end apart: 5, of which 4 were waited for; matrix products, arithmetic and copies ran while one was open for 19% of the time, Pallas kernels for 0%

commit v1 on v0

--- a/solution.py
+++ b/solution.py
@@ -69,7 +69,9 @@
     proj = jnp.einsum(
         "tn,cnw->ctw",
         columns,
-        lax.all_gather(proj_weight, "ctx", axis=1, tiled=True),
+        jnp.concatenate(
+            lax.all_to_all(jnp.stack([proj_weight] * lax.axis_size("ctx")), "ctx", 0, 0), axis=1
+        ),
         preferred_element_type=jnp.float32,
     )
     query_rows = normed(proj[0].reshape(-1, heads, head_dim), query_gain.reshape(heads, head_dim))

time: 202 us -> 379 us (1.88)
  waiting for transfers between devices: 135 us -> 289 us
  local copies, waits for them, and re-layouts: 23 us -> 36.5 us
  starting transfers between devices: 5.36 us -> 15.5 us
    all_to_all x0 -> x1, waiting for transfers between devices: none -> 220 us  [body(): lax.all_to_all(jnp.stack([proj_weight] * lax.axis_size('ctx')), 'ctx', 0, 0)]
    all_gather x1 -> x0, waiting for transfers between devices: 64 us -> none  [body(): lax.all_gather(proj_weight, 'ctx', axis=1, tiled=True)]
    all_to_all x0 -> x1, starting transfers between devices: none -> 10.1 us  [body(): lax.all_to_all(jnp.stack([proj_weight] * lax.axis_size('ctx')), 'ctx', 0, 0)]
    reshape x0 -> x1, local copies, waits for them, and re-layouts: none -> 9.08 us  [body(): jnp.concatenate(lax.all_to_all(jnp.stack([proj_weight] * lax.axis_size('c...]
    another operation x0 -> x1, local copies, waits for them, and re-layouts: none -> 5.15 us  [body(): jnp.stack([proj_weight] * lax.axis_size('ctx'))]
  transfers between devices with their start and end apart: 5 -> 5, of which waited for: 4 -> 4; matrix products, arithmetic and copies ran while one was open for 19% -> 13% of each run, Pallas kernels for 0% -> 0%
where the time goes in v1:
time: 379 us; the launch traced here: 378 us
  waiting for transfers between devices  289 us (76%)
  local copies, waits for them, and re-layouts  36.5 us (10%)
  matrix products  21.4 us (6%)
  starting transfers between devices  15.5 us (4%)
  between operations  13.6 us (4%)
    all_to_all x1, waiting for transfers between devices, body(): lax.all_to_all(jnp.stack([proj_weight] * lax.axis_size('ctx')), 'ctx', 0, 0)  220 us
    all_gather x1, waiting for transfers between devices, body(): lax.all_gather(attended, 'dp', axis=1, tiled=True)  62.1 us
    gather x3, local copies, waits for them, and re-layouts, attend(): lookup[indices]  12.7 us
    all_to_all x1, starting transfers between devices, body(): lax.all_to_all(jnp.stack([proj_weight] * lax.axis_size('ctx')), 'ctx', 0, 0)  10.1 us
    dot_general x1, matrix products, body(): jnp.einsum('tn,cnw->ctw', columns, jnp.concatenate(lax.all_to_all(jnp.sta...  9.53 us
    reshape x1, local copies, waits for them, and re-layouts, body(): jnp.concatenate(lax.all_to_all(jnp.stack([proj_weight] * lax.axis_size('c...  9.08 us
  transfers between devices with their start and end apart: 5, of which 4 were waited for; matrix products, arithmetic and copies ran while one was open for 13% of the time, Pallas kernels for 0%

profile of v1, /device:TPU:1, one launch (start us, length us, event | category | flops | bytes accessed | tf_op | source)
XLA Modules:
  0.0 378.1 jit_solution(3663708350910387252)
XLA Ops:
  6.5 1.4 copy.21
  7.9 5.2 %stack.4 = bf16[16,3,384,256]{2,3,1,0:T(8,128)(2,1)} broadcast(bf16[3,384,256]{1,2,0:T(8,128)(2,1)S(1)} %copy.21), dimensions={1,2,3} | broadcast | bytes 10027008 | tf_op jit(solution)/shard_map/stack | solution.py:73
  13.1 10.1 %all-to-all-start = ((bf16[16,3,384,256]{2,3,1,0:T(8,128)(2,1)}), bf16[16,3,384,256]{2,3,1,0:T(8,128)(2,1)}, u32[]{:S(2)}, u32[]{:S(2)}) async-start(bf16[16,3,384,256]{2,3,1,0:T(8,128)(2,1)} %stack.4), calls=%async_computation | async-start | bytes 18874368 | tf_op jit(solution)/shard_map/all_to_all | solution.py:73
  23.2 0.0 all-gather.5.cloned.1.call-start
  23.2 0.7 all-gather.5.cloned.1.call-update
  23.9 0.0 all-gather.3.cloned.1.call-start
  24.0 0.0 copy-done.1
  24.0 219.9 %all-to-all-done = bf16[16,3,384,256]{2,3,1,0:T(8,128)(2,1)} async-done(((bf16[16,3,384,256]{2,3,1,0:T(8,128)(2,1)}), bf16[16,3,384,256]{2,3,1,0:T(8,128)(2,1)}, u32[]{:S(2)}, u32[]{:S(2)}) %all-to-all-start) | async-done | bytes 9437216 | tf_op jit(solution)/shard_map/all_to_all | solution.py:73
  243.8 9.1 %copy.35 = bf16[16,3,32,8,384]{4,3,0,2,1:T(8,128)(2,1)} copy(bf16[16,3,32,8,384]{4,3,2,1,0:T(8,128)(2,1)} %bitcast.16) | data formatting | bytes 18874368 | tf_op jit(solution)/shard_map/reshape | solution.py:72
  252.9 9.5 %fusion.4 = f32[3,512,256]{1,2,0:T(8,128)S(1)} fusion(bf16[3,6144,256]{1,2,0:T(8,128)(2,1)} %bitcast.58, bf16[512,6144]{1,0:T(8,128)(2,1)} %param.7), kind=kOutput, calls=%fused_computation.9 | convolution fusion | flops 4831838208 | bytes 17301504 | tf_op jit(solution)/shard_map/tn,cnw->ctw/dot_general | solution.py:69
  262.5 0.0 copy-start.4
  262.5 0.0 copy-start.3
  262.6 0.1 reduce_sum.28
  262.6 0.0 copy-done.2
  262.6 0.2 slice_multiply_fusion.1
  262.9 0.1 pad_maximum_fusion.1
  262.9 2.4 collective-permute-start
  265.3 2.9 collective-permute-start.1
  268.2 0.0 copy-done.4
  268.2 0.1 fusion.24
  268.3 0.1 reshape.78
  268.4 0.1 broadcast_in_dim.5
  268.5 0.1 mul.100
  268.6 0.2 copy.23
  268.8 0.3 reshape_squeeze.10
  269.1 0.1 reduce_sum.27
  269.1 0.1 copy.24
  269.3 0.0 copy-done.3
  269.3 0.7 fusion.18
  270.0 1.4 collective-permute-done
  271.4 4.5 %collective-permute-done.1 = bf16[2,512,256]{1,2,0:T(8,128)(2,1)} collective-permute-done((bf16[2,512,256]{1,2,0:T(8,128)(2,1)S(1)}, bf16[2,512,256]{1,2,0:T(8,128)(2,1)}, u32[]{:S(2)}, u32[]{:S(2)}) %collective-permute-start.1) | collective-permute-done | bytes 524320 | tf_op jit(solution)/shard_map/ppermute | solution.py:18
  275.9 1.3 pad_maximum_fusion
  277.3 1.0 fusion.25
  278.2 0.9 reshape.98
  279.2 1.0 copy.26
  280.2 2.4 reshape.99
  282.6 1.0 copy.29
  283.5 6.4 %gather_fusion = bf16[288,64,128]{2,1,0:T(8,128)(2,1)} fusion(bf16[2,24,64,128]{3,2,1,0:T(8,128)(2,1)S(1)} %bitcast.56, s32[288]{0:T(512)S(1)} %reshape.78), kind=kCustom, calls=%fused_computation | custom fusion | bytes 9439488 | tf_op jit(solution)/shard_map/vmap()/gather | solution.py:36
  289.9 6.3 %gather_fusion.1 = bf16[288,64,128]{2,1,0:T(8,128)(2,1)} fusion(bf16[2,24,64,128]{3,2,1,0:T(8,128)(2,1)S(1)} %bitcast.57, s32[288]{0:T(512)S(1)} %reshape.78), kind=kCustom, calls=%fused_computation.1 | custom fusion | bytes 9439488 | tf_op jit(solution)/shard_map/vmap()/gather | solution.py:37
  296.2 4.5 %fusion.26 = (f32[2,8,64]{2,1,0:T(8,128)S(1)}, bf16[2,8,64,1152]{3,2,1,0:T(8,128)(2,1)S(1)}) fusion(f32[2,8,1152]{2,1,0:T(8,128)S(1)} %mul.100, bf16[2,8,1152,128]{3,2,1,0:T(8,128)(2,1)} %bitcast.60, bf16[2,8,64,128]{3,0,2,1:T(2,128)(2,1)S(1)} %fusion.18), kind=kOutput, calls=%fused_computation.35 | convolution fusion | flops 306707456 | bytes 7417856 | tf_op jit(solution)/shard_map/hqtd,hqsd->hqts/dot_general | solution.py:41
  300.7 0.0 copy-done
  300.7 1.1 fusion.13
  301.8 0.3 copy.30
  302.1 0.7 copy.42
  302.8 0.0 all-gather.3.cloned.1.call-update
  302.9 0.0 all-gather.5.cloned.1.call-done
  302.9 62.1 %all-gather.3.cloned.1.call-done = bf16[512,4096]{1,0:T(8,128)(2,1)} async-done(((bf16[512,256]{1,0:T(8,128)(2,1)}), bf16[512,4096]{1,0:T(8,128)(2,1)}) %all-gather.3.cloned.1.call-update) | async-done | bytes 4194320 | tf_op jit(solution)/shard_map/all_gather | solution.py:89
  365.0 6.3 %convolution_convert_fusion = bf16[512,384]{1,0:T(8,128)(2,1)} fusion(bf16[512,4096]{1,0:T(8,128)(2,1)} %all-gather.3.cloned.1.call-done, bf16[384,4096]{1,0:T(8,128)(2,1)} %all-gather.5.cloned.1.call-done), kind=kOutput, calls=%fused_computation.10 | convolution fusion | flops 1610809344 | bytes 7733248 | tf_op jit(solution)/shard_map/dot_general | solution.py:88
  (8 shorter events, 0.1 us)
Async XLA Ops:
  13.1 10.9 %copy-start.1 = (s32[2,8,18]{2,1,0:T(8,128)S(1)}, s32[2,8,18]{2,1,0:T(8,128)}, u32[]{:S(2)}) copy-start(s32[2,8,18]{2,1,0:T(8,128)} %param.12) | copy-start | bytes 3460
  13.1 230.8 %all-to-all-start = ((bf16[16,3,384,256]{2,3,1,0:T(8,128)(2,1)}), bf16[16,3,384,256]{2,3,1,0:T(8,128)(2,1)}, u32[]{:S(2)}, u32[]{:S(2)}) async-start(bf16[16,3,384,256]{2,3,1,0:T(8,128)(2,1)} %stack.4), calls=%async_computation | async-start | bytes 18874368 | tf_op jit(solution)/shard_map/all_to_all | solution.py:73
  23.2 279.7 %all-gather.5.cloned.1.call-start = ((), (), s32[]{:S(2)}) async-start(), calls=%async_computation.2 | async-start | bytes 3342336 | tf_op jit(solution)/shard_map/all_gather | solution.py:86
  23.9 341.1 %all-gather.3.cloned.1.call-start = ((), (), s32[]{:S(2)}) async-start(), calls=%async_computation.1 | async-start | bytes 4456448 | tf_op jit(solution)/shard_map/all_gather | solution.py:89
  252.9 9.7 %copy-start.2 = (f32[256]{0:T(256)S(1)}, f32[256]{0:T(256)}, u32[]{:S(2)}) copy-start(f32[256]{0:T(256)} %param.11) | copy-start | bytes 3076
  262.5 5.8 %copy-start.4 = (s32[2,8]{1,0:T(2,128)S(1)}, s32[2,8]{1,0:T(2,128)}, u32[]{:S(2)}) copy-start(s32[2,8]{1,0:T(2,128)} %param.13) | copy-start | bytes 196
  262.5 6.8 %copy-start.3 = (f32[256]{0:T(256)S(1)}, f32[256]{0:T(256)}, u32[]{:S(2)}) copy-start(f32[256]{0:T(256)} %param.10) | copy-start | bytes 3076
  262.9 8.5 %collective-permute-start = (bf16[2,512,256]{1,2,0:T(8,128)(2,1)S(1)}, bf16[2,512,256]{1,2,0:T(8,128)(2,1)}, u32[]{:S(2)}, u32[]{:S(2)}) collective-permute-start(bf16[2,512,256]{1,2,0:T(8,128)(2,1)S(1)} %pad_maximum_fusion.1), channel_id=1, source_target_pairs={{0,1},{1,2},{2,3},{3,4},{4,5},{5,6},{6,7},{7,8},{8,9},{9,10},{10,1... | collective-permute-start | bytes 1572872 | tf_op jit(solution)/shard_map/ppermute | solution.py:15
  265.3 10.6 %collective-permute-start.1 = (bf16[2,512,256]{1,2,0:T(8,128)(2,1)S(1)}, bf16[2,512,256]{1,2,0:T(8,128)(2,1)}, u32[]{:S(2)}, u32[]{:S(2)}) collective-permute-start(bf16[2,512,256]{1,2,0:T(8,128)(2,1)S(1)} %pad_maximum_fusion.1), channel_id=1, source_target_pairs={{1,0},{2,1},{3,2},{4,3},{5,4},{6,5},{7,6},{8,7},{9,8},{10,9},{11,1... | collective-permute-start | bytes 1572872 | tf_op jit(solution)/shard_map/ppermute | solution.py:18
  296.2 4.5 %copy-start = (bf16[288,64,128]{2,1,0:T(8,128)(2,1)S(1)}, bf16[288,64,128]{2,1,0:T(8,128)(2,1)}, u32[]{:S(2)}) copy-start(bf16[288,64,128]{2,1,0:T(8,128)(2,1)} %gather_fusion.1) | copy-start | bytes 14155780
Sparse Core Ops, SparseCore 0:
  25.8 112.1 all-gather.4
  303.0 61.9 all-gather.2
